TPU v7x, 32 devices: a whole 2x2x4 slice. The times are simulated.
32 devices in a mesh: comp: 2 (over x), lon: 8 (over z, core), ch: 2 (over y).
Axes of the slice: x: 2, y: 2, z: 4, core: 2. Of those that a mesh axis runs over, the one named last changes fastest.
Arguments:
- ocean_state: bfloat16 [3, 128, 64, 256], P(None, 'ch', ('comp', 'lon')), may hold values from -6 to 6
- ocean_mask: int32 [64, 256], P(('comp', 'lon')), may hold values 0 or 1
- air_state: bfloat16 [2, 192, 32, 2, 256], P(None, 'ch', 'lon', None, 'comp'), may hold values from -6 to 6
- surface_temp: float32 [64, 256], P(('comp', 'lon')), may hold values from -6 to 6
- air_fluxes: float32 [4, 32, 2, 256], P(None, 'lon', None, 'comp'), may hold values from -6 to 6
- ocean_kernel: float32 [128, 3, 7, 7], P('ch'), may hold values from -0.5 to 0.5
- ocean_gain: float32 [128], replicated, may hold values from 0.5 to 1.5
- ocean_up: bfloat16 [128, 512], replicated, may hold values from -0.5 to 0.5
- ocean_down: bfloat16 [512, 128], replicated, may hold values from -0.25 to 0.25
- air_kernel: float32 [192, 3, 7, 7], P('ch'), may hold values from -0.5 to 0.5
- air_gain: float32 [192], replicated, may hold values from 0.5 to 1.5
- air_up: bfloat16 [192, 768], replicated, may hold values from -0.4375 to 0.4375
- air_down: bfloat16 [768, 192], replicated, may hold values from -0.21875 to 0.21875
- flux_weight: float32 [4, 128], P(None, 'ch'), may hold values from -3 to 3
- temp_weight: float32 [192], P('ch'), may hold values from -1 to 1
Outputs:
- ocean_next: bfloat16 [3, 128, 64, 256], P(None, 'ch', ('comp', 'lon'))
- air_next: bfloat16 [2, 192, 32, 2, 256], P(None, 'ch', 'lon', None, 'comp')
All inputs are finite; a program needn't handle non-finite values. No bound on the sum of `ocean_mask` on one device may be relied on, other than what follows from the above.
Results may differ from a plain program's by a relative error of at most 0.007.
Values may be sent and summed in bfloat16 or wider, within the bound.
A program may use at most 64 MiB of HBM per device.

v0:
```python
import jax
import jax.numpy as jnp
from jax import lax
from jax.sharding import PartitionSpec as P


def padded_2(block, sides, width):
    for axis, dim in sides:
        count = lax.axis_size(axis)
        forward = [(i, i + 1) for i in range(count - 1)]
        forward.append((count - 1, 0))
        backward = [(target, source) for source, target in forward]
        low = lax.ppermute(
            lax.slice_in_dim(block, block.shape[dim] - width, None, axis=dim), axis, forward
        )
        high = lax.ppermute(lax.slice_in_dim(block, 0, width, axis=dim), axis, backward)
        block = jnp.concatenate([low, block, high], axis=dim)
    return block


def depthwise(padded, kernel, out_shape):
    levels = out_shape[0]
    widths = out_shape[2]
    lat_cells = out_shape[-1]
    ones_tail = (1,) * (padded.ndim - 2)
    summed = jnp.zeros(out_shape, jnp.float32)
    for level_off in range(3):
        for lon_off in range(7):
            for lat_off in range(7):
                weight = kernel[:, level_off, lon_off, lat_off].reshape(
                    (1, kernel.shape[0]) + ones_tail
                )
                window = lax.slice_in_dim(padded, level_off, level_off + levels, axis=0)
                window = lax.slice_in_dim(window, lon_off, lon_off + widths, axis=2)
                window = lax.slice_in_dim(
                    window, lat_off, lat_off + lat_cells, axis=padded.ndim - 1
                )
                summed = summed + weight * window
    return summed


def channel_norm(conv_out, gain_vec):
    values = conv_out.astype(jnp.float32)
    center = jnp.mean(values, axis=1, keepdims=True)
    spread = jnp.mean(jnp.square(values - center), axis=1, keepdims=True)
    scaled = gain_vec.reshape((1, gain_vec.shape[0]) + (1,) * (values.ndim - 2))
    return ((values - center) * lax.rsqrt(spread + 1e-06) * scaled).astype(jnp.bfloat16)


def feed_forward(normed, up_proj, down_proj):
    hidden = jax.nn.gelu(
        jnp.einsum("ch,lc...->lh...", up_proj, normed, preferred_element_type=jnp.float32)
    ).astype(jnp.bfloat16)
    return jnp.einsum("hc,lh...->lc...", down_proj, hidden, preferred_element_type=jnp.float32)


def mend_edges(edged, band_cells, lat_part, groups):
    row_index = jnp.arange(lat_part + 6)
    comp_index = lax.axis_index("comp")
    drop_rows = (row_index < 3) & (comp_index == 0) | (row_index >= lat_part + 3) & (
        comp_index == groups - 1
    )
    edged = jnp.where(drop_rows, 0.0, edged)
    column_index = jnp.arange(band_cells + 6)
    lon_index = lax.axis_index("lon")
    bands = lax.axis_size("lon")
    west_cols = ((column_index < 3) & (lon_index == 0))[:, None, None]
    east_cols = ((column_index >= band_cells + 3) & (lon_index == bands - 1))[:, None, None]
    return jnp.where(
        west_cols,
        jnp.roll(edged, 1, axis=3),
        jnp.where(east_cols, jnp.roll(edged, -1, axis=3), edged),
    )


def per_device(
    ocean_state,
    ocean_mask,
    air_state,
    surface_temp,
    air_fluxes,
    ocean_kernel,
    ocean_gain,
    ocean_up,
    ocean_down,
    air_kernel,
    air_gain,
    air_up,
    air_down,
    flux_weight,
    temp_weight,
):
    sea_mask = ocean_mask.astype(jnp.float32)
    band_cells = ocean_state.shape[2]
    lat_cells = ocean_state.shape[3]
    groups = lax.axis_size("comp")
    lat_part = lat_cells // groups
    flux_count = air_fluxes.shape[0]
    sent_temp = (surface_temp * sea_mask).reshape(1, band_cells, 1, groups, lat_part)
    sent_flux = air_fluxes.reshape(flux_count, band_cells, 1, groups, lat_part)
    got_temp, got_flux = (
        lax.all_to_all(sent_temp, "comp", split_axis=3, concat_axis=2, tiled=True),
        lax.all_to_all(sent_flux, "comp", split_axis=3, concat_axis=2, tiled=True),
    )
    air_temp = got_temp.reshape(band_cells, groups, lat_part)
    ocean_flux = got_flux.reshape(flux_count, band_cells, lat_cells)
    surface_stack = jnp.concatenate([ocean_flux, sea_mask[None]], axis=0)
    state_rimmed = padded_2(ocean_state, ((("comp", "lon"), 2),), 3)
    surface_rimmed = padded_2(surface_stack, ((("comp", "lon"), 1),), 3)
    sea_rimmed = surface_rimmed[flux_count]
    inject_rimmed = jnp.einsum(
        "kc,kxy->cxy", flux_weight, surface_rimmed[:flux_count], precision=lax.Precision.HIGHEST
    )
    state_wide = state_rimmed.astype(jnp.float32)
    rimmed = (
        jnp.concatenate([state_wide[:1] + inject_rimmed[None], state_wide[1:]], axis=0) * sea_rimmed
    )
    ocean_forced = rimmed[:, :, 3 : 3 + band_cells]
    air_rimmed = padded_2(air_state, (("comp", 4), ("lon", 2)), 3)
    temp_rimmed = padded_2(air_temp, (("comp", 2), ("lon", 0)), 3)
    air_wide = air_rimmed.astype(jnp.float32)
    heating_wide = temp_weight[:, None, None, None] * temp_rimmed[None]
    edged = jnp.concatenate([air_wide[:1] + heating_wide[None], air_wide[1:]], axis=0)
    edged = mend_edges(edged, band_cells, lat_part, groups)
    air_forced = edged[:, :, 3 : 3 + band_cells, :, 3 : 3 + lat_part]
    rimmed = jnp.pad(rimmed, ((1, 1), (0, 0), (0, 0), (3, 3)))
    ocean_conv = depthwise(rimmed, ocean_kernel, ocean_forced.shape).astype(jnp.bfloat16)
    edged = jnp.pad(edged, ((1, 1), (0, 0), (0, 0), (0, 0), (0, 0)))
    air_conv = depthwise(edged, air_kernel, air_forced.shape).astype(jnp.bfloat16)
    whole_ocean, whole_air = (
        lax.all_gather(ocean_conv, "ch", axis=1, tiled=True),
        lax.all_gather(air_conv, "ch", axis=1, tiled=True),
    )
    part_index = lax.axis_index("ch")
    parts = lax.axis_size("ch")
    ocean_width = ocean_up.shape[1] // parts
    air_width = air_up.shape[1] // parts
    ocean_part = feed_forward(
        channel_norm(whole_ocean, ocean_gain),
        lax.dynamic_slice_in_dim(ocean_up, part_index * ocean_width, ocean_width, 1),
        lax.dynamic_slice_in_dim(ocean_down, part_index * ocean_width, ocean_width, 0),
    )
    air_part = feed_forward(
        channel_norm(whole_air, air_gain),
        lax.dynamic_slice_in_dim(air_up, part_index * air_width, air_width, 1),
        lax.dynamic_slice_in_dim(air_down, part_index * air_width, air_width, 0),
    )
    ocean_summed, air_summed = (
        lax.psum_scatter(ocean_part, "ch", scatter_dimension=1, tiled=True),
        lax.psum_scatter(air_part, "ch", scatter_dimension=1, tiled=True),
    )
    ocean_update = ocean_summed.astype(jnp.bfloat16)
    air_update = air_summed.astype(jnp.bfloat16)
    ocean_next = ((ocean_forced + ocean_update.astype(jnp.float32)) * sea_mask).astype(jnp.bfloat16)
    air_next = (air_forced + air_update.astype(jnp.float32)).astype(jnp.bfloat16)
    return (ocean_next, air_next)


def solution(mesh):
    in_specs = (
        P(None, "ch", ("comp", "lon"), None),
        P(("comp", "lon"), None),
        P(None, "ch", "lon", None, "comp"),
        P(("comp", "lon"), None),
        P(None, "lon", None, "comp"),
        P("ch", None, None, None),
        P(),
        P(),
        P(),
        P("ch", None, None, None),
        P(),
        P(),
        P(),
        P(None, "ch"),
        P("ch"),
    )
    out_specs = (P(None, "ch", ("comp", "lon"), None), P(None, "ch", "lon", None, "comp"))
    return jax.shard_map(
        per_device, mesh=mesh, in_specs=in_specs, out_specs=out_specs, check_vma=False
    )
```

profile of v0, /device:TPU:0, one launch (start us, length us, event | category | flops | bytes accessed | tf_op | source)
XLA Modules:
  0.0 230.6 jit_solution(2810779744101454819)
XLA Ops:
  7.2 1.1 copy.36
  8.4 0.9 fusion.609
  9.3 2.9 %collective-permute-start.4 = (bf16[2,96,4,2,3]{4,1,3,2,0:T(8,128)(2,1)}, bf16[2,96,4,2,3]{4,1,3,2,0:T(8,128)(2,1)S(1)}, u32[]{:S(2)}, u32[]{:S(2)}) collective-permute-start(bf16[2,96,4,2,3]{4,1,3,2,0:T(8,128)(2,1)} %get-tuple-element.12), channel_id=1, source_target_pairs={{0,16},{16,0},{1,17},{17,1},{2,18},{18,2},{3,19},{19,3},{4,20},{20... | collective-permute-start | bytes 27656 | tf_op jit(solution)/shard_map/ppermute | solution.py:13
  12.9 3.3 %all-to-all-start.1 = ((f32[1,4,1,2,128]{4,1,2,0,3:T(4,128)}), f32[1,4,1,2,128]{4,1,2,0,3:T(4,128)S(1)}, u32[]{:S(2)}, u32[]{:S(2)}) async-start(f32[1,4,1,2,128]{4,1,2,0,3:T(4,128)} %multiply_bitcast_fusion), calls=%async_computation.2 | async-start | bytes 8192 | tf_op jit(solution)/shard_map/all_to_all | solution.py:102
  16.2 0.9 fusion.610
  17.1 0.7 slice_bitcast_fusion.142
  17.7 0.7 slice_bitcast_fusion.141
  18.4 0.7 slice_bitcast_fusion.20
  19.0 0.7 slice_bitcast_fusion.146
  19.7 0.6 slice_bitcast_fusion.145
  20.4 0.7 slice_bitcast_fusion.144
  21.0 0.7 slice_bitcast_fusion.143
  21.7 0.6 slice_bitcast_fusion.140
  22.3 0.7 slice_bitcast_fusion.292
  23.0 0.7 slice_bitcast_fusion.291
  23.7 0.7 slice_bitcast_fusion.290
  24.3 0.7 slice_bitcast_fusion.289
  25.0 0.6 slice_bitcast_fusion.288
  25.7 0.7 slice_bitcast_fusion.167
  26.3 0.6 slice_bitcast_fusion.287
  28.6 4.6 %all-to-all-done.1 = f32[1,4,1,2,128]{4,1,2,0,3:T(4,128)S(1)} async-done(((f32[1,4,1,2,128]{4,1,2,0,3:T(4,128)}), f32[1,4,1,2,128]{4,1,2,0,3:T(4,128)S(1)}, u32[]{:S(2)}, u32[]{:S(2)}) %all-to-all-start.1) | async-done | bytes 4128 | tf_op jit(solution)/shard_map/all_to_all | solution.py:102
  33.2 3.2 %all-to-all-start = ((f32[4,4,1,2,128]{4,1,0,2,3:T(4,128)}), f32[4,4,1,2,128]{4,1,0,2,3:T(4,128)S(1)}, u32[]{:S(2)}, u32[]{:S(2)}) async-start(f32[4,4,1,2,128]{4,1,0,2,3:T(4,128)} %bitcast.645), calls=%async_computation | async-start | bytes 32768 | tf_op jit(solution)/shard_map/all_to_all | solution.py:103
  36.6 2.0 collective-permute-start.8
  38.6 1.7 collective-permute-done.8
  40.3 1.8 collective-permute-done.9
  42.3 3.5 %collective-permute-start.11 = (f32[3,2,134]{2,0,1:T(4,128)S(1)}, f32[3,2,134]{2,0,1:T(4,128)S(1)}, u32[]{:S(2)}, u32[]{:S(2)}) collective-permute-start(f32[3,2,134]{2,0,1:T(4,128)S(1)} %get-tuple-element.313), channel_id=1, source_target_pairs={{2,0},{4,2},{6,4},{8,6},{10,8},{12,10},{14,12},{0,14},{3,1},{5,3},... | collective-permute-start | bytes 9656 | tf_op jit(solution)/shard_map/ppermute | solution.py:16
  45.8 1.4 collective-permute-done.10
  48.0 3.9 %collective-permute-start.3 = (f32[5,3,256]{2,0,1:T(8,128)S(1)}, f32[5,3,256]{2,0,1:T(8,128)S(1)}, u32[]{:S(2)}, u32[]{:S(2)}) collective-permute-start(f32[5,3,256]{2,0,1:T(8,128)S(1)} %get-tuple-element.311), channel_id=1, source_target_pairs={{2,0},{4,2},{6,4},{8,6},{10,8},{12,10},{14,12},{16,14},{18,16},{20... | collective-permute-start | bytes 46088 | tf_op jit(solution)/shard_map/ppermute | solution.py:16
  51.9 0.7 copy-done.2
  53.3 1.2 copy.39
  54.5 1.2 copy.40
  55.7 3.5 %collective-permute-start.7 = (bf16[2,96,3,2,134]{1,3,4,2,0:T(2,128)(2,1)}, bf16[2,96,3,2,134]{1,3,4,2,0:T(2,128)(2,1)}, u32[]{:S(2)}, u32[]{:S(2)}) collective-permute-start(bf16[2,96,3,2,134]{1,3,4,2,0:T(2,128)(2,1)} %copy.40), channel_id=1, source_target_pairs={{2,0},{4,2},{6,4},{8,6},{10,8},{12,10},{14,12},{0,14},{3,1},{5,3},... | collective-permute-start | bytes 926216 | tf_op jit(solution)/shard_map/ppermute | solution.py:16
  59.4 0.7 convert_add_fusion
  61.2 29.4 %fusion.522 = bf16[3,64,4,256]{3,1,2,0:T(8,128)(2,1)S(1)} fusion(f32[3,64,10,256]{3,1,2,0:T(8,128)S(1)} %maximum_multiply_fusion, f32[64]{0:T(128)} %get-tuple-element.289, f32[64]{0:T(128)} %get-tuple-element.290, f32[64]{0:T(128)} %get-tuple-element.292, f32[64]{0:T(128)} %get-tuple-element.293, f32[64]{0:T(128)} %get-tuple-element.294, ...), kind=kLoop, calls=%fused_computation.768 | loop fusion | flops 57802752 | bytes 7917312 | tf_op jit(solution)/shard_map/convert_element_type | solution.py:127
  90.6 8.7 %all_gather.6 = bf16[3,128,4,256]{3,1,2,0:T(8,128)(2,1)S(1)} all-gather(bf16[3,64,4,256]{3,1,2,0:T(8,128)(2,1)S(1)} %fusion.522), channel_id=1, replica_groups=mesh['comp'=2,'lon'=8,'ch'=2] {'ch'}, dimensions={1}, use_global_device_ids=true | all-gather | bytes 1179648 | tf_op jit(solution)/shard_map/all_gather | solution.py:131
  99.7 3.8 %fusion.29 = f32[3,128,4,256]{3,1,2,0:T(8,128)} fusion(bf16[3,128,4,256]{3,1,2,0:T(8,128)(2,1)S(1)} %all_gather.6, f32[128]{0:T(128)} %param.21, f32[3,4,256]{2,1,0:T(4,128)S(1)} %add_rsqrt_fusion, f32[3,4,256]{2,1,0:T(4,128)S(1)} %broadcast_multiply_fusion, bf16[512,128]{1,0:T(8,128)(2,1)} %param.23, s32[]{:T(128)S(6)} %select_n.19, ...), kind=kOutput, calls=%fused_computation.278 | convolution fusion | flops 411697152 | bytes 2516480 | tf_op jit(solution)/shard_map/hc,lh...->lc.../dot_general | solution.py:54
  103.8 1.4 copy.41
  105.2 2.1 copy.42
  107.2 2.2 maximum_convert_fusion
  110.8 3.5 %select_select_fusion = f32[2,96,10,2,134]{4,1,3,2,0:T(8,128)} fusion(f32[2,96,10,1,134]{4,1,3,2,0:T(8,128)S(1)} %get-tuple-element.7, f32[2,96,10,1,134]{4,1,3,2,0:T(8,128)S(1)} %get-tuple-element.6, pred[10]{0:T(512)(128)(4,1)} %compare_and_fusion, pred[10]{0:T(512)(128)(4,1)} %compare_and_fusion.1, f32[1,96,10,2,134]{4,1,3,2,0:T(8,128)S(1)} %get-tuple-element.9, ...), kind=kLoop, calls=%fused_computation.238 | loop fusion | flops 2572800 | bytes 6174874 | tf_op jit(solution)/shard_map/jit(_where)/select_n | solution.py:69
  114.6 65.0 %fusion.576 = bf16[2,96,4,2,128]{4,1,3,2,0:T(8,128)(2,1)S(1)} fusion(f32[2,96,10,2,134]{4,1,3,2,0:T(8,128)} %select_select_fusion, f32[96]{0:T(128)} %get-tuple-element.142, f32[96]{0:T(128)} %get-tuple-element.143, f32[96]{0:T(128)} %get-tuple-element.145, f32[96]{0:T(128)} %get-tuple-element.146, f32[96]{0:T(128)} %get-tuple-element.147, ...), kind=kLoop, calls=%fused_computation.873 | loop fusion | flops 57802752 | bytes 42930816 | tf_op jit(solution)/shard_map/convert_element_type | solution.py:129
  179.7 8.7 %all_gather.7 = bf16[2,192,4,2,128]{4,1,3,2,0:T(8,128)(2,1)S(1)} all-gather(bf16[2,96,4,2,128]{4,1,3,2,0:T(8,128)(2,1)S(1)} %fusion.576), channel_id=1, replica_groups=mesh['comp'=2,'lon'=8,'ch'=2] {'ch'}, dimensions={1}, use_global_device_ids=true | all-gather | bytes 1179648 | tf_op jit(solution)/shard_map/all_gather | solution.py:132
  188.7 3.7 %fusion.27 = f32[2,192,4,2,128]{4,1,3,2,0:T(8,128)} fusion(bf16[2,192,4,2,128]{4,1,3,2,0:T(8,128)(2,1)S(1)} %all_gather.7, f32[192]{0:T(256)} %param.25, f32[2,4,2,128]{3,2,1,0:T(2,128)S(1)} %add_rsqrt_fusion.1, f32[2,4,2,128]{3,2,1,0:T(2,128)S(1)} %broadcast_multiply_fusion.1, bf16[768,192]{0,1:T(8,128)(2,1)S(1)} %copy-done, s32[]{:T(128)S(6)} %select_n.23, ...), kind=kOutput, calls=%fused_computation.276 | convolution fusion | flops 613023744 | bytes 2672640 | tf_op jit(solution)/shard_map/hc,lh...->lc.../dot_general | solution.py:54
  192.5 1.3 multiply_convert_fusion
  193.7 1.1 copy.46
  194.8 26.0 %reduce-scatter.5.cloned.1.call-done = f32[2,96,4,2,128]{4,1,3,2,0:T(8,128)} async-done(((f32[2,192,4,2,128]{4,1,3,2,0:T(8,128)}), f32[2,96,4,2,128]{4,1,3,2,0:T(8,128)}) %reduce-scatter.5.cloned.1.call-update) | async-done | bytes 786448 | tf_op jit(solution)/shard_map/reduce_scatter | solution.py:150
  220.8 1.9 add_convert_fusion
  222.7 1.0 copy.47
  (234 shorter events, 7.1 us)
Async XLA Ops:
  7.2 181.6 %copy-start = (bf16[768,192]{0,1:T(8,128)(2,1)S(1)}, bf16[768,192]{0,1:T(8,128)(2,1)}, u32[]{:S(2)}) copy-start(bf16[768,192]{0,1:T(8,128)(2,1)} %param.27) | copy-start | bytes 884740
  7.2 5.1 %copy-start.6 = (s32[4,256]{1,0:T(4,128)S(1)}, s32[4,256]{1,0:T(4,128)}, u32[]{:S(2)}) copy-start(s32[4,256]{1,0:T(4,128)} %param.16) | copy-start | bytes 12292
  7.2 5.1 %copy-start.8 = (f32[4,256]{1,0:T(4,128)S(1)}, f32[4,256]{1,0:T(4,128)}, u32[]{:S(2)}) copy-start(f32[4,256]{1,0:T(4,128)} %param.18) | copy-start | bytes 12292
  7.2 8.9 %copy-start.3 = (bf16[3,64,4,256]{3,2,1,0:T(4,128)(2,1)S(1)}, bf16[3,64,4,256]{3,2,1,0:T(4,128)(2,1)}, u32[]{:S(2)}) copy-start(bf16[3,64,4,256]{3,2,1,0:T(4,128)(2,1)} %param.15) | copy-start | bytes 1179652
  8.3 8.7 %copy-start.4 = (f32[96,3,7,7]{0,3,2,1:T(8,128)S(1)}, f32[96,3,7,7]{0,3,2,1:T(8,128)}, u32[]{:S(2)}) copy-start(f32[96,3,7,7]{0,3,2,1:T(8,128)} %param.24) | copy-start | bytes 169348
  8.3 14.0 %copy-start.5 = (f32[64,3,7,7]{0,3,2,1:T(8,128)S(1)}, f32[64,3,7,7]{0,3,2,1:T(8,128)}, u32[]{:S(2)}) copy-start(f32[64,3,7,7]{0,3,2,1:T(8,128)} %param.20) | copy-start | bytes 112900
  8.3 19.6 %copy-start.7 = (f32[4,4,2,128]{3,2,1,0:T(2,128)S(1)}, f32[4,4,2,128]{3,2,1,0:T(2,128)}, u32[]{:S(2)}) copy-start(f32[4,4,2,128]{3,2,1,0:T(2,128)} %param.19) | copy-start | bytes 49156
  9.3 38.7 %collective-permute-start.4 = (bf16[2,96,4,2,3]{4,1,3,2,0:T(8,128)(2,1)}, bf16[2,96,4,2,3]{4,1,3,2,0:T(8,128)(2,1)S(1)}, u32[]{:S(2)}, u32[]{:S(2)}) collective-permute-start(bf16[2,96,4,2,3]{4,1,3,2,0:T(8,128)(2,1)} %get-tuple-element.12), channel_id=1, source_target_pairs={{0,16},{16,0},{1,17},{17,1},{2,18},{18,2},{3,19},{19,3},{4,20},{20... | collective-permute-start | bytes 27656 | tf_op jit(solution)/shard_map/ppermute | solution.py:13
  12.2 39.7 %collective-permute-start.5 = (bf16[2,96,4,2,3]{4,1,3,2,0:T(8,128)(2,1)S(1)}, bf16[2,96,4,2,3]{4,1,3,2,0:T(8,128)(2,1)S(1)}, u32[]{:S(2)}, u32[]{:S(2)}) collective-permute-start(bf16[2,96,4,2,3]{4,1,3,2,0:T(8,128)(2,1)S(1)} %get-tuple-element.13), channel_id=1, source_target_pairs={{16,0},{0,16},{17,1},{1,17},{18,2},{2,18},{19,3},{3,19},{20,4},{4,... | collective-permute-start | bytes 27656 | tf_op jit(solution)/shard_map/ppermute | solution.py:16
  12.9 20.3 %all-to-all-start.1 = ((f32[1,4,1,2,128]{4,1,2,0,3:T(4,128)}), f32[1,4,1,2,128]{4,1,2,0,3:T(4,128)S(1)}, u32[]{:S(2)}, u32[]{:S(2)}) async-start(f32[1,4,1,2,128]{4,1,2,0,3:T(4,128)} %multiply_bitcast_fusion), calls=%async_computation.2 | async-start | bytes 8192 | tf_op jit(solution)/shard_map/all_to_all | solution.py:102
  17.1 42.2 %collective-permute-start = (bf16[3,64,3,256]{3,1,2,0:T(8,128)(2,1)}, bf16[3,64,3,256]{3,1,2,0:T(8,128)(2,1)S(1)}, u32[]{:S(2)}, u32[]{:S(2)}) collective-permute-start(bf16[3,64,3,256]{3,1,2,0:T(8,128)(2,1)} %get-tuple-element.14), channel_id=1, source_target_pairs={{0,2},{2,4},{4,6},{6,8},{8,10},{10,12},{12,14},{14,16},{16,18},{18... | collective-permute-start | bytes 884744 | tf_op jit(solution)/shard_map/ppermute | solution.py:13
  33.2 14.2 %all-to-all-start = ((f32[4,4,1,2,128]{4,1,0,2,3:T(4,128)}), f32[4,4,1,2,128]{4,1,0,2,3:T(4,128)S(1)}, u32[]{:S(2)}, u32[]{:S(2)}) async-start(f32[4,4,1,2,128]{4,1,0,2,3:T(4,128)} %bitcast.645), calls=%async_computation | async-start | bytes 32768 | tf_op jit(solution)/shard_map/all_to_all | solution.py:103
  36.4 156.0 %reduce-scatter.3.cloned.1.call-start = ((), (), s32[]{:S(2)}) async-start(), calls=%async_computation.4 | async-start | bytes 2359296 | tf_op jit(solution)/shard_map/reduce_scatter | solution.py:149
  36.6 3.8 %collective-permute-start.8 = (f32[4,2,3]{2,0,1:T(4,128)S(1)}, f32[4,2,3]{2,0,1:T(4,128)S(1)}, u32[]{:S(2)}, u32[]{:S(2)}) collective-permute-start(f32[4,2,3]{2,0,1:T(4,128)S(1)} %get-tuple-element.314), channel_id=1, source_target_pairs={{0,16},{16,0},{1,17},{17,1},{2,18},{18,2},{3,19},{19,3},{4,20},{20... | collective-permute-start | bytes 296 | tf_op jit(solution)/shard_map/ppermute | solution.py:13
  38.5 3.6 %collective-permute-start.9 = (f32[4,2,3]{2,0,1:T(4,128)S(1)}, f32[4,2,3]{2,0,1:T(4,128)S(1)}, u32[]{:S(2)}, u32[]{:S(2)}) collective-permute-start(f32[4,2,3]{2,0,1:T(4,128)S(1)} %get-tuple-element.315), channel_id=1, source_target_pairs={{16,0},{0,16},{17,1},{1,17},{18,2},{2,18},{19,3},{3,19},{20,4},{4,... | collective-permute-start | bytes 296 | tf_op jit(solution)/shard_map/ppermute | solution.py:16
  42.2 5.0 %collective-permute-start.10 = (f32[3,2,134]{2,0,1:T(4,128)S(1)}, f32[3,2,134]{2,0,1:T(4,128)S(1)}, u32[]{:S(2)}, u32[]{:S(2)}) collective-permute-start(f32[3,2,134]{2,0,1:T(4,128)S(1)} %get-tuple-element.312), channel_id=1, source_target_pairs={{0,2},{2,4},{4,6},{6,8},{8,10},{10,12},{12,14},{14,0},{1,3},{3,5},... | collective-permute-start | bytes 9656 | tf_op jit(solution)/shard_map/ppermute | solution.py:13
  42.3 5.0 %collective-permute-start.11 = (f32[3,2,134]{2,0,1:T(4,128)S(1)}, f32[3,2,134]{2,0,1:T(4,128)S(1)}, u32[]{:S(2)}, u32[]{:S(2)}) collective-permute-start(f32[3,2,134]{2,0,1:T(4,128)S(1)} %get-tuple-element.313), channel_id=1, source_target_pairs={{2,0},{4,2},{6,4},{8,6},{10,8},{12,10},{14,12},{0,14},{3,1},{5,3},... | collective-permute-start | bytes 9656 | tf_op jit(solution)/shard_map/ppermute | solution.py:16
  47.2 12.1 %collective-permute-start.1 = (bf16[3,64,3,256]{3,1,2,0:T(8,128)(2,1)}, bf16[3,64,3,256]{3,1,2,0:T(8,128)(2,1)S(1)}, u32[]{:S(2)}, u32[]{:S(2)}) collective-permute-start(bf16[3,64,3,256]{3,1,2,0:T(8,128)(2,1)} %get-tuple-element.15), channel_id=1, source_target_pairs={{2,0},{4,2},{6,4},{8,6},{10,8},{12,10},{14,12},{16,14},{18,16},{20... | collective-permute-start | bytes 884744 | tf_op jit(solution)/shard_map/ppermute | solution.py:16
  47.4 8.2 %collective-permute-start.2 = (f32[5,3,256]{2,0,1:T(8,128)S(1)}, f32[5,3,256]{2,0,1:T(8,128)S(1)}, u32[]{:S(2)}, u32[]{:S(2)}) collective-permute-start(f32[5,3,256]{2,0,1:T(8,128)S(1)} %get-tuple-element.310), channel_id=1, source_target_pairs={{0,2},{2,4},{4,6},{6,8},{8,10},{10,12},{12,14},{14,16},{16,18},{18... | collective-permute-start | bytes 46088 | tf_op jit(solution)/shard_map/ppermute | solution.py:13
  48.0 3.9 %copy-start.1 = (bf16[2,96,4,2,3]{4,1,3,2,0:T(8,128)(2,1)}, bf16[2,96,4,2,3]{4,1,3,2,0:T(8,128)(2,1)S(1)}, u32[]{:S(2)}) copy-start(bf16[2,96,4,2,3]{4,1,3,2,0:T(8,128)(2,1)S(1)} %collective-permute-done.4) | copy-start | bytes 27652
  48.0 11.2 %collective-permute-start.3 = (f32[5,3,256]{2,0,1:T(8,128)S(1)}, f32[5,3,256]{2,0,1:T(8,128)S(1)}, u32[]{:S(2)}, u32[]{:S(2)}) collective-permute-start(f32[5,3,256]{2,0,1:T(8,128)S(1)} %get-tuple-element.311), channel_id=1, source_target_pairs={{2,0},{4,2},{6,4},{8,6},{10,8},{12,10},{14,12},{16,14},{18,16},{20... | collective-permute-start | bytes 46088 | tf_op jit(solution)/shard_map/ppermute | solution.py:16
  54.5 4.9 %copy-start.9 = (f32[4,64]{1,0:T(4,128)S(1)}, f32[4,64]{1,0:T(4,128)}, u32[]{:S(2)}) copy-start(f32[4,64]{1,0:T(4,128)} %param.28) | copy-start | bytes 3076
  54.5 49.3 %collective-permute-start.6 = (bf16[2,96,3,2,134]{1,3,4,2,0:T(2,128)(2,1)}, bf16[2,96,3,2,134]{1,3,4,2,0:T(2,128)(2,1)}, u32[]{:S(2)}, u32[]{:S(2)}) collective-permute-start(bf16[2,96,3,2,134]{1,3,4,2,0:T(2,128)(2,1)} %copy.39), channel_id=1, source_target_pairs={{0,2},{2,4},{4,6},{6,8},{8,10},{10,12},{12,14},{14,0},{1,3},{3,5},... | collective-permute-start | bytes 926216 | tf_op jit(solution)/shard_map/ppermute | solution.py:13
  55.7 49.5 %collective-permute-start.7 = (bf16[2,96,3,2,134]{1,3,4,2,0:T(2,128)(2,1)}, bf16[2,96,3,2,134]{1,3,4,2,0:T(2,128)(2,1)}, u32[]{:S(2)}, u32[]{:S(2)}) collective-permute-start(bf16[2,96,3,2,134]{1,3,4,2,0:T(2,128)(2,1)} %copy.40), channel_id=1, source_target_pairs={{2,0},{4,2},{6,4},{8,6},{10,8},{12,10},{14,12},{0,14},{3,1},{5,3},... | collective-permute-start | bytes 926216 | tf_op jit(solution)/shard_map/ppermute | solution.py:16
  103.5 117.3 %reduce-scatter.5.cloned.1.call-start = ((), (), s32[]{:S(2)}) async-start(), calls=%async_computation.5 | async-start | bytes 2359296 | tf_op jit(solution)/shard_map/reduce_scatter | solution.py:150
  110.4 3.8 %copy-start.49 = (f32[96]{0:T(128)S(1)}, f32[96]{0:T(128)}, u32[]{:S(2)}) copy-start(f32[96]{0:T(128)} %get-tuple-element.92) | copy-start | bytes 1156
  110.4 3.8 %copy-start.50 = (f32[96]{0:T(128)S(1)}, f32[96]{0:T(128)}, u32[]{:S(2)}) copy-start(f32[96]{0:T(128)} %get-tuple-element.93) | copy-start | bytes 1156
  110.5 3.8 %copy-start.51 = (f32[96]{0:T(128)S(1)}, f32[96]{0:T(128)}, u32[]{:S(2)}) copy-start(f32[96]{0:T(128)} %get-tuple-element.94) | copy-start | bytes 1156
  110.5 3.8 %copy-start.52 = (f32[96]{0:T(128)S(1)}, f32[96]{0:T(128)}, u32[]{:S(2)}) copy-start(f32[96]{0:T(128)} %get-tuple-element.95) | copy-start | bytes 1156
  110.5 3.8 %copy-start.53 = (f32[96]{0:T(128)S(1)}, f32[96]{0:T(128)}, u32[]{:S(2)}) copy-start(f32[96]{0:T(128)} %get-tuple-element.96) | copy-start | bytes 1156
  110.5 3.8 %copy-start.54 = (f32[96]{0:T(128)S(1)}, f32[96]{0:T(128)}, u32[]{:S(2)}) copy-start(f32[96]{0:T(128)} %get-tuple-element.97) | copy-start | bytes 1156
  110.5 3.8 %copy-start.55 = (f32[96]{0:T(128)S(1)}, f32[96]{0:T(128)}, u32[]{:S(2)}) copy-start(f32[96]{0:T(128)} %get-tuple-element.98) | copy-start | bytes 1156
  110.5 3.8 %copy-start.56 = (f32[96]{0:T(128)S(1)}, f32[96]{0:T(128)}, u32[]{:S(2)}) copy-start(f32[96]{0:T(128)} %get-tuple-element.99) | copy-start | bytes 1156
  110.5 3.8 %copy-start.57 = (f32[96]{0:T(128)S(1)}, f32[96]{0:T(128)}, u32[]{:S(2)}) copy-start(f32[96]{0:T(128)} %get-tuple-element.100) | copy-start | bytes 1156
  110.5 3.8 %copy-start.58 = (f32[96]{0:T(128)S(1)}, f32[96]{0:T(128)}, u32[]{:S(2)}) copy-start(f32[96]{0:T(128)} %get-tuple-element.101) | copy-start | bytes 1156
  110.5 3.8 %copy-start.59 = (f32[96]{0:T(128)S(1)}, f32[96]{0:T(128)}, u32[]{:S(2)}) copy-start(f32[96]{0:T(128)} %get-tuple-element.102) | copy-start | bytes 1156
  110.5 3.8 %copy-start.60 = (f32[96]{0:T(128)S(1)}, f32[96]{0:T(128)}, u32[]{:S(2)}) copy-start(f32[96]{0:T(128)} %get-tuple-element.103) | copy-start | bytes 1156
  110.6 3.8 %copy-start.61 = (f32[96]{0:T(128)S(1)}, f32[96]{0:T(128)}, u32[]{:S(2)}) copy-start(f32[96]{0:T(128)} %get-tuple-element.104) | copy-start | bytes 1156
  110.6 3.8 %copy-start.62 = (f32[96]{0:T(128)S(1)}, f32[96]{0:T(128)}, u32[]{:S(2)}) copy-start(f32[96]{0:T(128)} %get-tuple-element.105) | copy-start | bytes 1156
  110.6 3.8 %copy-start.63 = (f32[96]{0:T(128)S(1)}, f32[96]{0:T(128)}, u32[]{:S(2)}) copy-start(f32[96]{0:T(128)} %get-tuple-element.106) | copy-start | bytes 1156
  110.6 3.8 %copy-start.64 = (f32[96]{0:T(128)S(1)}, f32[96]{0:T(128)}, u32[]{:S(2)}) copy-start(f32[96]{0:T(128)} %get-tuple-element.107) | copy-start | bytes 1156
  110.6 3.8 %copy-start.65 = (f32[96]{0:T(128)S(1)}, f32[96]{0:T(128)}, u32[]{:S(2)}) copy-start(f32[96]{0:T(128)} %get-tuple-element.108) | copy-start | bytes 1156
  110.6 3.8 %copy-start.66 = (f32[96]{0:T(128)S(1)}, f32[96]{0:T(128)}, u32[]{:S(2)}) copy-start(f32[96]{0:T(128)} %get-tuple-element.109) | copy-start | bytes 1156
  110.6 3.8 %copy-start.67 = (f32[96]{0:T(128)S(1)}, f32[96]{0:T(128)}, u32[]{:S(2)}) copy-start(f32[96]{0:T(128)} %get-tuple-element.110) | copy-start | bytes 1156
  110.6 3.8 %copy-start.68 = (f32[96]{0:T(128)S(1)}, f32[96]{0:T(128)}, u32[]{:S(2)}) copy-start(f32[96]{0:T(128)} %get-tuple-element.111) | copy-start | bytes 1156
  110.6 3.8 %copy-start.69 = (f32[96]{0:T(128)S(1)}, f32[96]{0:T(128)}, u32[]{:S(2)}) copy-start(f32[96]{0:T(128)} %get-tuple-element.112) | copy-start | bytes 1156
  110.6 3.8 %copy-start.70 = (f32[96]{0:T(128)S(1)}, f32[96]{0:T(128)}, u32[]{:S(2)}) copy-start(f32[96]{0:T(128)} %get-tuple-element.113) | copy-start | bytes 1156
  110.7 3.8 %copy-start.71 = (f32[96]{0:T(128)S(1)}, f32[96]{0:T(128)}, u32[]{:S(2)}) copy-start(f32[96]{0:T(128)} %get-tuple-element.114) | copy-start | bytes 1156
  (57 other events, 90.0 us)
Sparse Core Ops, SparseCore 0:
  103.7 24.7 reduce-scatter.2
  192.6 28.1 reduce-scatter.4
where the time goes:
time: 231 us
  other arithmetic  107 us (46%)
  waiting for transfers between devices  35.6 us (15%)
  starting transfers between devices  23.4 us (10%)
  local copies, waits for them, and re-layouts  23.3 us (10%)
  blocking collectives  17.4 us (8%)
  between operations  15.4 us (7%)
  matrix products  8.21 us (4%)
    convert_element_type x1, other arithmetic, per_device(): depthwise(edged, air_kernel, air_forced.shape).astype(jnp.bfloat16)  65 us
    convert_element_type x1, other arithmetic, per_device(): depthwise(rimmed, ocean_kernel, ocean_forced.shape).astype(jnp.bfloat16)  29.4 us
    reduce_scatter x1, waiting for transfers between devices, per_device(): lax.psum_scatter(air_part, 'ch', scatter_dimension=1, tiled=True)  26 us
    ppermute x6, starting transfers between devices, padded_2(): lax.ppermute(lax.slice_in_dim(block, 0, width, axis=dim), axis, backward)  11.1 us
    mul x16, local copies, waits for them, and re-layouts, depthwise(): summed = summed + weight * window  9.86 us
    all_gather x1, blocking collectives, per_device(): lax.all_gather(ocean_conv, 'ch', axis=1, tiled=True)  8.69 us
    all_gather x1, blocking collectives, per_device(): lax.all_gather(air_conv, 'ch', axis=1, tiled=True)  8.67 us
    dot_general x2, matrix products, feed_forward(): jnp.einsum('hc,lh...->lc...', down_proj, hidden, preferred_element_type=j...  7.48 us
  transfers between devices with their start and end apart: 16, of which 5 were waited for; matrix products, arithmetic and copies ran while one was open for 57% of the time, Pallas kernels for 0%

commit v1 on v0

v1 whole, which is shorter than its diff:
```python
import functools

import jax
import jax.numpy as jnp
from jax import lax
from jax.experimental import pallas as pl
from jax.experimental.pallas import tpu as pltpu
from jax.sharding import PartitionSpec as P

LANES = 128
ROWS = 16
HALF = 8


def conv_taps(main, wrap, k_ref, rows, p, levels, width):
    lane = lax.broadcasted_iota(jnp.int32, (width + 6, HALF, LANES), 2)
    sums = [None] * levels
    for d in range(7):
        s = d - 3
        shifted = []
        for lev in range(levels):
            v = main[lev, p, :, rows, :]
            if s > 0:
                v = pltpu.roll(jnp.where(lane < s, wrap[lev, p], v), LANES - s, 2)
            elif s < 0:
                v = pltpu.roll(jnp.where(lane >= LANES + s, wrap[lev, p], v), -s, 2)
            shifted.append(v)
        for a in range(3):
            for b in range(7):
                tap = a * 49 + b * 7 + d
                w = jnp.broadcast_to(k_ref[rows, tap : tap + 1], (HALF, LANES))[None]
                for lev in range(levels):
                    src = lev + a - 1
                    if 0 <= src < levels:
                        term = w * shifted[src][b : b + width]
                        sums[lev] = term if sums[lev] is None else sums[lev] + term
    return sums


def ocean_conv_kernel(x_ref, k_ref, o_ref, main, wrap, total):
    levels, wide, _, lat = x_ref.shape
    tiles = lat // LANES
    width = wide - 6
    lane = lax.broadcasted_iota(jnp.int32, (wide, HALF, LANES), 2)
    for lev in range(levels):
        for p in range(tiles):
            main[lev, p] = x_ref[lev, :, :, p * LANES : (p + 1) * LANES].astype(jnp.float32)

    def body(sub, carry):
        rows = pl.ds(pl.multiple_of(sub * HALF, HALF), HALF)
        zero = jnp.zeros((wide, HALF, LANES), jnp.float32)
        for p in range(tiles):
            for lev in range(levels):
                high = main[lev, p + 1, :, rows, :] if p + 1 < tiles else zero
                low = main[lev, p - 1, :, rows, :] if p > 0 else zero
                wrap[lev, p] = jnp.where(lane < LANES // 2, high, low)
        for p in range(tiles):
            sums = conv_taps(main, wrap, k_ref, rows, p, levels, width)
            for lev in range(levels):
                total[lev, p, :, rows, :] = sums[lev]
        return carry

    lax.fori_loop(0, ROWS // HALF, body, 0)
    for lev in range(levels):
        for p in range(tiles):
            o_ref[lev, :, :, p * LANES : (p + 1) * LANES] = total[lev, p].astype(jnp.bfloat16)


def air_conv_kernel(x_ref, e_ref, k_ref, o_ref, main, wrap, total, edge):
    levels, halves, wide, _, _ = x_ref.shape
    width = wide - 6
    for lev in range(levels):
        edge[lev] = e_ref[lev].astype(jnp.float32)
        for p in range(halves):
            main[lev, p] = x_ref[lev, p].astype(jnp.float32)

    def body(sub, carry):
        rows = pl.ds(pl.multiple_of(sub * HALF, HALF), HALF)
        for lev in range(levels):
            e = edge[lev, rows, :]
            for p in range(halves):
                for m in range(wide):
                    base = (p * wide + m) * 6 + 3
                    wrap[lev, p, m] = pltpu.roll(e, LANES - base, 1)
        for p in range(halves):
            sums = conv_taps(main, wrap, k_ref, rows, p, levels, width)
            for lev in range(levels):
                total[lev, p, :, rows, :] = sums[lev]
        return carry

    lax.fori_loop(0, ROWS // HALF, body, 0)
    for lev in range(levels):
        for p in range(halves):
            o_ref[lev, p] = total[lev, p].astype(jnp.bfloat16)


def conv_scratch(levels, tiles, wide):
    return [
        pltpu.VMEM((levels, tiles, wide, ROWS, LANES), jnp.float32),
        pltpu.VMEM((levels, tiles, wide, HALF, LANES), jnp.float32),
        pltpu.VMEM((levels, tiles, wide - 6, ROWS, LANES), jnp.float32),
    ]


def ocean_conv(x, k):
    levels, wide, ch, lat = x.shape
    return pl.pallas_call(
        ocean_conv_kernel,
        grid=(ch // ROWS,),
        in_specs=[
            pl.BlockSpec((levels, wide, ROWS, lat), lambda g: (0, 0, g, 0)),
            pl.BlockSpec((ROWS, k.shape[1]), lambda g: (g, 0)),
        ],
        out_specs=pl.BlockSpec((levels, wide - 6, ROWS, lat), lambda g: (0, 0, g, 0)),
        out_shape=jax.ShapeDtypeStruct((levels, wide - 6, ch, lat), jnp.bfloat16),
        scratch_shapes=conv_scratch(levels, lat // LANES, wide),
        compiler_params=pltpu.CompilerParams(vmem_limit_bytes=32 * 1024 * 1024),
        cost_estimate=pl.CostEstimate(
            flops=25_000_000, bytes_accessed=1_500_000, transcendentals=0
        ),
    )(x, k)


def air_conv(x, e, k):
    levels, halves, wide, ch, lat = x.shape
    return pl.pallas_call(
        air_conv_kernel,
        grid=(ch // ROWS,),
        in_specs=[
            pl.BlockSpec((levels, halves, wide, ROWS, lat), lambda g: (0, 0, 0, g, 0)),
            pl.BlockSpec((levels, ROWS, LANES), lambda g: (0, g, 0)),
            pl.BlockSpec((ROWS, k.shape[1]), lambda g: (g, 0)),
        ],
        out_specs=pl.BlockSpec((levels, halves, wide - 6, ROWS, lat), lambda g: (0, 0, 0, g, 0)),
        out_shape=jax.ShapeDtypeStruct((levels, halves, wide - 6, ch, lat), jnp.bfloat16),
        scratch_shapes=conv_scratch(levels, halves, wide)
        + [pltpu.VMEM((levels, ROWS, LANES), jnp.float32)],
        compiler_params=pltpu.CompilerParams(vmem_limit_bytes=32 * 1024 * 1024),
        cost_estimate=pl.CostEstimate(
            flops=20_000_000, bytes_accessed=1_500_000, transcendentals=0
        ),
    )(x, e, k)


def mlp_kernel(mine_ref, other_ref, res_ref, gain_ref, up_ref, down_ref, sea_ref, o_ref):
    count = mine_ref.shape[1]

    def wide(ref):
        return jnp.concatenate([ref[0, i] for i in range(count)], axis=1)

    values = jnp.concatenate([wide(mine_ref), wide(other_ref)], axis=0).astype(jnp.float32)
    center = jnp.mean(values, axis=0, keepdims=True)
    moved = values - center
    spread = jnp.mean(moved * moved, axis=0, keepdims=True)
    normed = (moved * lax.rsqrt(spread + 1e-06) * gain_ref[...]).astype(jnp.bfloat16)
    raw = jnp.dot(up_ref[...], normed, preferred_element_type=jnp.float32)
    hidden = jax.nn.gelu(raw).astype(jnp.bfloat16)
    update = jnp.dot(down_ref[...], hidden, preferred_element_type=jnp.float32)
    update = update.astype(jnp.bfloat16).astype(jnp.float32)
    out = wide(res_ref).astype(jnp.float32) + update
    lat = mine_ref.shape[3]
    for i in range(count):
        piece = out[:, i * lat : (i + 1) * lat]
        if sea_ref is not None:
            piece = piece * sea_ref[i : i + 1, :].astype(jnp.float32)
        o_ref[0, i] = piece.astype(jnp.bfloat16)


def mlp(mine, other, resid, gain, up, down, sea, count):
    lead, cols, ch, lat = mine.shape
    block = pl.BlockSpec((1, count, ch, lat), lambda i, j: (i, j, 0, 0))
    whole = lambda arr: pl.BlockSpec(arr.shape, lambda i, j: (0,) * arr.ndim)
    ins = [mine, other, resid, gain, up, down]
    specs = [block, block, block, whole(gain), whole(up), whole(down)]
    kernel = mlp_kernel
    if sea is None:
        kernel = lambda m, t, r, g, u, d, o: mlp_kernel(m, t, r, g, u, d, None, o)
    else:
        ins.append(sea)
        specs.append(whole(sea))
    return pl.pallas_call(
        kernel,
        grid=(lead, cols // count),
        in_specs=specs,
        out_specs=block,
        out_shape=jax.ShapeDtypeStruct(mine.shape, jnp.bfloat16),
        compiler_params=pltpu.CompilerParams(vmem_limit_bytes=32 * 1024 * 1024),
        cost_estimate=pl.CostEstimate(
            flops=600_000_000, bytes_accessed=2_000_000, transcendentals=1_500_000
        ),
    )(*ins)


def ring(axis):
    count = lax.axis_size(axis)
    forward = [(i, (i + 1) % count) for i in range(count)]
    return forward, [(t, s) for s, t in forward]


def per_device(
    ocean_state,
    ocean_mask,
    air_state,
    surface_temp,
    air_fluxes,
    ocean_kernel,
    ocean_gain,
    ocean_up,
    ocean_down,
    air_kernel,
    air_gain,
    air_up,
    air_down,
    flux_weight,
    temp_weight,
):
    f32, bf16 = jnp.float32, jnp.bfloat16
    comp = lax.axis_index("comp")
    lon = lax.axis_index("lon")
    bands = lax.axis_size("lon")
    swap = [(0, 1), (1, 0)]
    first = comp == 0
    band = ocean_state.shape[2]
    lat = ocean_state.shape[3]
    part = air_state.shape[4]
    air_lev, air_ch = air_state.shape[:2]

    sea = ocean_mask.astype(f32)
    own_temp = surface_temp * sea
    own_flux = jnp.where(first, air_fluxes[:, :, 0], air_fluxes[:, :, 1])
    sent_flux = jnp.where(first, air_fluxes[:, :, 1], air_fluxes[:, :, 0])
    sent_edge = jnp.where(first, air_state[..., -3:], air_state[..., :3])
    sent_edge = jnp.transpose(sent_edge, (0, 1, 3, 2, 4)).reshape(air_lev, air_ch, -1)
    got_temp = lax.ppermute(own_temp, "comp", swap)
    got_flux = lax.ppermute(sent_flux, "comp", swap)
    got_edge = lax.ppermute(sent_edge, "comp", swap)

    flux = jnp.where(
        first,
        jnp.concatenate([own_flux, got_flux], axis=-1),
        jnp.concatenate([got_flux, own_flux], axis=-1),
    )
    state = jnp.transpose(ocean_state, (0, 2, 1, 3)).astype(f32)
    inject = sum(
        flux_weight[k][None, :, None] * flux[k][:, None, :] for k in range(flux.shape[0])
    )
    forced = jnp.concatenate([state[:1] + inject[None], state[1:]], axis=0)
    forced = (forced * sea[None, :, None, :]).astype(bf16)
    forward, backward = ring(("comp", "lon"))
    west = lax.ppermute(forced[:, -3:], ("comp", "lon"), forward)
    east = lax.ppermute(forced[:, :3], ("comp", "lon"), backward)

    temp = jnp.where(first, jnp.stack([own_temp, got_temp]), jnp.stack([got_temp, own_temp]))
    temp = jnp.pad(temp, ((0, 0), (0, 0), (3, 3)))
    temp = lax.dynamic_slice_in_dim(temp, comp * part, part + 6, 2)
    air = jnp.transpose(air_state, (0, 3, 2, 1, 4)).astype(f32)
    heat = temp_weight[None, None, :, None] * temp[:, :, None, 3 : 3 + part]
    air = jnp.concatenate([air[:1] + heat[None], air[1:]], axis=0).astype(bf16)
    got_edge = got_edge.reshape(air_lev, air_ch, 2, band, 3).astype(f32)
    zero = jnp.zeros_like(got_edge)
    edge = jnp.where(
        first,
        jnp.concatenate([zero, got_edge], axis=-1),
        jnp.concatenate([got_edge, zero], axis=-1),
    )
    rim = jnp.concatenate([temp[:, :, :3], temp[:, :, -3:]], axis=-1)
    rim = temp_weight[:, None, None, None] * rim[None]
    edge = jnp.concatenate([edge[:1] + rim[None], edge[1:]], axis=0).astype(bf16)
    forward, backward = ring("lon")
    air_west = lax.ppermute(air[:, :, -3:], "lon", forward)
    air_east = lax.ppermute(air[:, :, :3], "lon", backward)
    edge_shape = (air_lev, air_ch, -1)
    edge_west = lax.ppermute(edge[:, :, :, -3:].reshape(edge_shape), "lon", forward)
    edge_east = lax.ppermute(edge[:, :, :, :3].reshape(edge_shape), "lon", backward)
    halo_shape = (air_lev, air_ch, 2, 3, 6)
    edge_west = edge_west.reshape(halo_shape)
    edge_east = edge_east.reshape(halo_shape)
    at_west, at_east = lon == 0, lon == bands - 1
    air_west = jnp.where(at_west, air_west[:, ::-1], air_west)
    air_east = jnp.where(at_east, air_east[:, ::-1], air_east)
    edge_west = jnp.where(at_west, edge_west[:, :, ::-1], edge_west)
    edge_east = jnp.where(at_east, edge_east[:, :, ::-1], edge_east)

    forced_wide = jnp.concatenate([west, forced, east], axis=1)
    ocean_mine = ocean_conv(forced_wide, ocean_kernel.reshape(ocean_kernel.shape[0], -1))
    ocean_other = lax.ppermute(ocean_mine, "ch", swap)
    air_wide = jnp.concatenate([air_west, air, air_east], axis=2)
    edges = jnp.concatenate([edge_west, edge, edge_east], axis=3).reshape(edge_shape)
    edges = jnp.pad(edges, ((0, 0), (0, 0), (0, LANES - edges.shape[-1])))
    air_mine = air_conv(air_wide, edges, air_kernel.reshape(air_kernel.shape[0], -1))
    air_other = lax.ppermute(air_mine, "ch", swap)

    at = lax.axis_index("ch")

    def mine_first(array, axis):
        low, high = jnp.split(array, 2, axis=axis)
        return jnp.where(
            at == 0,
            jnp.concatenate([low, high], axis=axis),
            jnp.concatenate([high, low], axis=axis),
        )

    def mine_only(array):
        low, high = jnp.split(array, 2, axis=1)
        return jnp.where(at == 0, low, high).T

    ocean_next = mlp(
        ocean_mine,
        ocean_other,
        forced,
        mine_first(ocean_gain, 0)[:, None],
        mine_first(ocean_up, 0).T,
        mine_only(ocean_down),
        ocean_mask,
        band,
    )
    flat = lambda v: v.reshape((air_lev * 2,) + v.shape[2:])
    air_next = mlp(
        flat(air_mine),
        flat(air_other),
        flat(air),
        mine_first(air_gain, 0)[:, None],
        mine_first(air_up, 0).T,
        mine_only(air_down),
        None,
        band,
    )
    air_next = air_next.reshape(air.shape)
    return jnp.transpose(ocean_next, (0, 2, 1, 3)), jnp.transpose(air_next, (0, 3, 2, 1, 4))


def solution(mesh):
    in_specs = (
        P(None, "ch", ("comp", "lon"), None),
        P(("comp", "lon"), None),
        P(None, "ch", "lon", None, "comp"),
        P(("comp", "lon"), None),
        P(None, "lon", None, "comp"),
        P("ch", None, None, None),
        P(),
        P(),
        P(),
        P("ch", None, None, None),
        P(),
        P(),
        P(),
        P(None, "ch"),
        P("ch"),
    )
    out_specs = (P(None, "ch", ("comp", "lon"), None), P(None, "ch", "lon", None, "comp"))
    return jax.shard_map(
        per_device, mesh=mesh, in_specs=in_specs, out_specs=out_specs, check_vma=False
    )
```

time: 231 us -> 74.5 us (0.32)
  other arithmetic: 107 us -> 6.45 us
  Pallas kernels: 0 us -> 30.2 us
  waiting for transfers between devices: 35.6 us -> 7.08 us
  blocking collectives: 17.4 us -> 0 us
  between operations: 15.4 us -> 1.13 us
  local copies, waits for them, and re-layouts: 23.3 us -> 11.7 us
  matrix products: 8.21 us -> 0 us
  starting transfers between devices: 23.4 us -> 17.5 us
    convert_element_type x7 -> x6, other arithmetic: 99.8 us -> 0.28 us  [the longest x1 0.08 us: per_device(): forced = (forced * sea[None, :, None, :]).astype(bf16)]
    pallas_call x0 -> x4, Pallas kernels: none -> 30.2 us  [the longest x1 12.2 us: air_conv(): pl.pallas_call(air_conv_kernel, grid=(ch // ROWS,), in_specs=[pl.BlockSpe...]
    reduce_scatter x2 -> x0, waiting for transfers between devices: 26 us -> none  [the longest x1 26 us: per_device(): lax.psum_scatter(air_part, 'ch', scatter_dimension=1, tiled=True)]
    all_gather x2 -> x0, blocking collectives: 17.4 us -> none  [the longest x1 8.69 us: per_device(): lax.all_gather(ocean_conv, 'ch', axis=1, tiled=True)]
    mul x16 -> x2, local copies, waits for them, and re-layouts: 9.86 us -> 0.52 us  [per_device(): flux_weight[k][None, :, None] * flux[k][:, None, :]]
    dot_general x3 -> x0, matrix products: 8.21 us -> none  [the longest x2 7.48 us: feed_forward(): jnp.einsum('hc,lh...->lc...', down_proj, hidden, preferred_element_type=j...]
    all_to_all x2 -> x0, starting transfers between devices: 6.5 us -> none  [the longest x1 3.26 us: per_device(): lax.all_to_all(sent_temp, 'comp', split_axis=3, concat_axis=2, tiled=True)]
    all_to_all x2 -> x0, waiting for transfers between devices: 4.59 us -> none  [the longest x1 4.59 us: per_device(): lax.all_to_all(sent_temp, 'comp', split_axis=3, concat_axis=2, tiled=True)]
  transfers between devices with their start and end apart: 16 -> 11, of which waited for: 5 -> 2; matrix products, arithmetic and copies ran while one was open for 57% -> 16% of each run, Pallas kernels for 0% -> 36%
where the time goes in v1:
time: 74.5 us; the launch traced here: 74.1 us
  Pallas kernels  30.2 us (41%)
  starting transfers between devices  17.5 us (23%)
  local copies, waits for them, and re-layouts  11.7 us (16%)
  waiting for transfers between devices  7.08 us (10%)
  other arithmetic  6.45 us (9%)
  between operations  1.13 us (2%)
    pallas_call x1, Pallas kernels, air_conv(): pl.pallas_call(air_conv_kernel, grid=(ch // ROWS,), in_specs=[pl.BlockSpe...  12.2 us
    pallas_call x1, Pallas kernels, ocean_conv(): pl.pallas_call(ocean_conv_kernel, grid=(ch // ROWS,), in_specs=[pl.BlockS...  10.9 us
    pallas_call x2, Pallas kernels, mlp(): pl.pallas_call(kernel, grid=(lead, cols // count), in_specs=specs, out_sp...  7.1 us
    ppermute x1, waiting for transfers between devices, per_device(): lax.ppermute(edge[:, :, :, -3:].reshape(edge_shape), 'lon', forward)  6.25 us
    unnamed x37, local copies, waits for them, and re-layouts  5.95 us
    ppermute x1, starting transfers between devices, per_device(): east = lax.ppermute(forced[:, :3], ('comp', 'lon'), backward)  4.44 us
    ppermute x1, starting transfers between devices, per_device(): lax.ppermute(edge[:, :, :, :3].reshape(edge_shape), 'lon', backward)  3.59 us
    ppermute x1, starting transfers between devices, per_device(): got_temp = lax.ppermute(own_temp, 'comp', swap)  2.94 us
  transfers between devices with their start and end apart: 11, of which 2 were waited for; matrix products, arithmetic and copies ran while one was open for 16% of the time, Pallas kernels for 36%

profile of v1, /device:TPU:0, one launch (start us, length us, event | category | flops | bytes accessed | tf_op | source)
XLA Modules:
  0.0 74.1 jit_solution(7104665379353914664)
XLA Ops:
  0.6 0.7 convert_multiply_fusion
  1.3 2.9 %collective-permute-start.4 = (f32[4,256]{1,0:T(4,128)S(1)}, f32[4,256]{1,0:T(4,128)S(1)}, u32[]{:S(2)}, u32[]{:S(2)}) collective-permute-start(f32[4,256]{1,0:T(4,128)S(1)} %convert_multiply_fusion), channel_id=1, source_target_pairs={{0,16},{16,0},{1,17},{17,1},{2,18},{18,2},{3,19},{19,3},{4,20},{20... | collective-permute-start | bytes 12296 | tf_op jit(solution)/shard_map/ppermute | solution.py:234
  4.3 1.9 %fusion.1 = bf16[2,96,2,4,3]{4,2,3,1,0:T(2,128)(2,1)S(1)} fusion(pred[]{:T(512)S(6)} %eq.8, bf16[2,96,4,2,128]{4,3,2,1,0:T(2,128)(2,1)} %param.17), kind=kLoop, calls=%fused_computation.10 | loop fusion | flops 4608 | bytes 27649 | tf_op jit(solution)/shard_map/transpose | solution.py:233
  6.1 0.5 copy.49
  6.7 2.1 %collective-permute-start = (f32[4,4,128]{2,1,0:T(4,128)S(1)}, f32[4,4,128]{2,1,0:T(4,128)S(1)}, u32[]{:S(2)}, u32[]{:S(2)}) collective-permute-start(f32[4,4,128]{2,1,0:T(4,128)S(1)} %bitcast.78), channel_id=1, source_target_pairs={{0,16},{16,0},{1,17},{17,1},{2,18},{18,2},{3,19},{19,3},{4,20},{20... | collective-permute-start | bytes 24584 | tf_op jit(solution)/shard_map/ppermute | solution.py:235
  8.9 0.2 copy.54
  9.1 0.7 %fusion.7 = (bf16[96,768]{0,1:T(8,128)(2,1)S(1)}, bf16[96,768]{0,1:T(8,128)(2,1)}) fusion(bf16[192,768]{0,1:T(8,128)(2,1)S(1)} %copy.54), kind=kLoop, calls=%fused_computation.51 | loop fusion | bytes 589824 | tf_op jit(solution)/shard_map/split | solution.py:296
  9.9 0.6 copy-done.14
  10.5 0.5 slice_bitcast_fusion.7
  11.1 0.8 %copy-done.7 = bf16[128,512]{1,0:T(8,128)(2,1)S(1)} copy-done((bf16[128,512]{1,0:T(8,128)(2,1)S(1)}, bf16[128,512]{1,0:T(8,128)(2,1)}, u32[]{:S(2)}) %copy-start.7) | copy-done | bytes 131096
  12.0 0.1 copy.44
  12.1 0.1 fusion.11
  12.2 0.8 %copy-done.3 = bf16[512,128]{1,0:T(8,128)(2,1)S(1)} copy-done((bf16[512,128]{1,0:T(8,128)(2,1)S(1)}, bf16[512,128]{1,0:T(8,128)(2,1)}, u32[]{:S(2)}) %copy-start.3) | copy-done | bytes 131096
  13.0 0.1 fusion.10
  13.1 0.1 copy.59
  13.2 0.1 copy.60
  13.3 0.7 %copy-done.5 = bf16[768,192]{0,1:T(8,128)(2,1)S(1)} copy-done((bf16[768,192]{0,1:T(8,128)(2,1)S(1)}, bf16[768,192]{0,1:T(8,128)(2,1)}, u32[]{:S(2)}) %copy-start.5) | copy-done | bytes 294936
  14.2 0.1 fusion.3.up_ref
  14.4 0.6 copy-done.11
  15.0 0.2 copy-done.8
  15.2 0.1 copy.51.k_ref
  15.3 0.8 %slice.120 = f32[2,4,64,256]{3,2,1,0:T(8,128)} slice(f32[3,4,64,256]{3,2,1,0:T(8,128)S(1)} %convert_bitcast_fusion.1), slice={[1:3], [0:4], [0:64], [0:256]} | slice | bytes 1048576 | tf_op jit(solution)/shard_map/slice | solution.py:247
  16.4 0.6 copy-done.13
  17.0 0.1 slice_add_fusion
  17.3 2.3 %collective-permute-start.6 = (bf16[2,2,3,96,128]{4,3,2,1,0:T(8,128)(2,1)S(1)}, bf16[2,2,3,96,128]{4,3,2,1,0:T(8,128)(2,1)S(1)}, u32[]{:S(2)}, u32[]{:S(2)}) collective-permute-start(bf16[2,2,3,96,128]{4,3,2,1,0:T(8,128)(2,1)S(1)} %get-tuple-element.11), channel_id=1, source_target_pairs={{2,0},{4,2},{6,4},{8,6},{10,8},{12,10},{14,12},{0,14},{3,1},{5,3},... | collective-permute-start | bytes 884744 | tf_op jit(solution)/shard_map/ppermute | solution.py:271
  19.7 0.2 slice_add_fusion.1
  20.1 0.1 fusion.4
  20.2 0.1 fusion.5
  20.3 3.6 %collective-permute-start.9 = (bf16[2,96,36]{1,0,2:T(2,128)(2,1)S(1)}, bf16[2,96,36]{1,0,2:T(2,128)(2,1)S(1)}, u32[]{:S(2)}, u32[]{:S(2)}) collective-permute-start(bf16[2,96,36]{1,0,2:T(2,128)(2,1)S(1)} %bitcast.74), channel_id=1, source_target_pairs={{2,0},{4,2},{6,4},{8,6},{10,8},{12,10},{14,12},{0,14},{3,1},{5,3},... | collective-permute-start | bytes 41480 | tf_op jit(solution)/shard_map/ppermute | solution.py:274
  23.9 0.9 %fusion.9 = (bf16[3,3,64,256]{3,2,1,0:T(8,128)(2,1)}, bf16[3,3,64,256]{3,2,1,0:T(8,128)(2,1)}) fusion(bf16[3,4,64,256]{3,2,1,0:T(8,128)(2,1)S(1)} %fusion.res_ref), kind=kLoop, calls=%fused_computation.53 | loop fusion | bytes 1179648 | tf_op jit(solution)/shard_map/slice | solution.py:250
  24.8 4.4 %collective-permute-start.2 = (bf16[3,3,64,256]{3,2,1,0:T(8,128)(2,1)}, bf16[3,3,64,256]{3,2,1,0:T(8,128)(2,1)}, u32[]{:S(2)}, u32[]{:S(2)}) collective-permute-start(bf16[3,3,64,256]{3,2,1,0:T(8,128)(2,1)} %get-tuple-element.13), channel_id=1, source_target_pairs={{2,0},{4,2},{6,4},{8,6},{10,8},{12,10},{14,12},{16,14},{18,16},{20... | collective-permute-start | bytes 884744 | tf_op jit(solution)/shard_map/ppermute | solution.py:251
  29.2 6.2 %collective-permute-done.8 = bf16[2,96,36]{1,0,2:T(2,128)(2,1)S(1)} collective-permute-done((bf16[2,96,36]{1,0,2:T(2,128)(2,1)S(1)}, bf16[2,96,36]{1,0,2:T(2,128)(2,1)S(1)}, u32[]{:S(2)}, u32[]{:S(2)}) %collective-permute-start.8) | collective-permute-done | bytes 13856 | tf_op jit(solution)/shard_map/ppermute | solution.py:273
  35.5 0.1 pad_maximum_fusion.2
  35.6 0.1 copy.50
  35.9 0.1 pad_maximum_fusion.1.x_ref
  36.1 12.2 %shard_map.160 = bf16[2,2,4,96,128]{4,3,2,1,0:T(8,128)(2,1)S(1)} custom-call(bf16[2,2,10,96,128]{4,3,2,1,0:T(8,128)(2,1)S(1)} %pad_maximum_fusion.1.x_ref, bf16[2,96,128]{2,1,0:T(8,128)(2,1)S(1)} %pad.11.e_ref, f32[96,147]{1,0:T(8,128)S(1)} %copy.51.k_ref), custom_call_target="tpu_custom_call" | custom-call | flops 20000000 | bytes 1500000 | tf_op jit(solution)/shard_map/pallas_call | solution.py:126
  48.3 1.6 %collective-permute-start.10 = (bf16[2,2,4,96,128]{4,3,2,1,0:T(8,128)(2,1)S(1)}, bf16[2,2,4,96,128]{4,3,2,1,0:T(8,128)(2,1)S(1)}, u32[]{:S(2)}, u32[]{:S(2)}) collective-permute-start(bf16[2,2,4,96,128]{4,3,2,1,0:T(8,128)(2,1)S(1)} %shard_map.160), channel_id=1, source_target_pairs={{0,1},{1,0},{2,3},{3,2},{4,5},{5,4},{6,7},{7,6},{8,9},{9,8},{10,11... | collective-permute-start | bytes 1179656 | tf_op jit(solution)/shard_map/ppermute | solution.py:291
  49.9 1.2 %pad_maximum_fusion.x_ref = bf16[3,10,64,256]{3,2,1,0:T(8,128)(2,1)S(1)} fusion(bf16[3,3,64,256]{3,2,1,0:T(8,128)(2,1)} %collective-permute-done.2, bf16[3,4,64,256]{3,2,1,0:T(8,128)(2,1)S(1)} %fusion.res_ref, bf16[3,3,64,256]{3,2,1,0:T(8,128)(2,1)} %collective-permute-done.1), kind=kLoop, calls=%fused_computation | loop fusion | flops 983040 | bytes 1966080 | tf_op jit(solution)/shard_map/concatenate | solution.py:284
  51.0 10.9 %shard_map.158.mine_ref = bf16[3,4,64,256]{3,2,1,0:T(8,128)(2,1)S(1)} custom-call(bf16[3,10,64,256]{3,2,1,0:T(8,128)(2,1)S(1)} %pad_maximum_fusion.x_ref, f32[64,147]{1,0:T(8,128)S(1)} %copy.41.k_ref), custom_call_target="tpu_custom_call" | custom-call | flops 25000000 | bytes 1500000 | tf_op jit(solution)/shard_map/pallas_call | solution.py:107
  61.9 0.6 collective-permute-start.3
  62.6 0.1 copy.55.g
  62.7 0.1 copy.47.gain_ref
  62.8 1.1 %fusion.2.u = bf16[768,192]{1,0:T(8,128)(2,1)S(1)} fusion(bf16[192,768]{0,1:T(8,128)(2,1)S(1)} %copy.54, bf16[96,768]{0,1:T(8,128)(2,1)} %get-tuple-element.9, bf16[96,768]{0,1:T(8,128)(2,1)S(1)} %get-tuple-element.8, pred[]{:T(512)S(6)} %eq.18), kind=kLoop, calls=%fused_computation.13 | loop fusion | flops 737280 | bytes 884737 | tf_op jit(solution)/shard_map/transpose | solution.py:323
  63.9 3.8 %shard_map.161 = bf16[4,4,96,128]{3,2,1,0:T(8,128)(2,1)S(1)} custom-call(bf16[4,4,96,128]{3,2,1,0:T(8,128)(2,1)S(1)} %bitcast.65, bf16[4,4,96,128]{3,2,1,0:T(8,128)(2,1)S(1)} %bitcast.66, bf16[4,4,96,128]{3,2,1,0:T(8,128)(2,1)S(1)} %bitcast.62, f32[192,1]{1,0:T(8,128)S(1)} %copy.55.g, bf16[768,192]{1,0:T(8,128)(2,1)S(1)} %fusion.2.u, ...), custom_call_target="tpu_custom_call" | custom-call | flops 600000000 | bytes 2000000 | tf_op jit(solution)/shard_map/pallas_call | solution.py:181
  67.8 1.2 %copy.64 = bf16[2,2,4,96,128]{4,1,2,3,0:T(2,128)(2,1)} copy(bf16[2,2,4,96,128]{4,3,2,1,0:T(8,128)(2,1)S(1)} %bitcast.63) | data formatting | bytes 786432 | tf_op jit(solution)/shard_map/reshape | solution.py:328
  68.9 0.8 %collective-permute-done.3.other_ref = bf16[3,4,64,256]{3,2,1,0:T(8,128)(2,1)S(1)} collective-permute-done((bf16[3,4,64,256]{3,2,1,0:T(8,128)(2,1)S(1)}, bf16[3,4,64,256]{3,2,1,0:T(8,128)(2,1)S(1)}, u32[]{:S(2)}, u32[]{:S(2)}) %collective-permute-start.3) | collective-permute-done | bytes 393248 | tf_op jit(solution)/shard_map/ppermute | solution.py:286
  69.8 3.3 %shard_map.159 = bf16[3,4,64,256]{3,2,1,0:T(8,128)(2,1)S(1)} custom-call(bf16[3,4,64,256]{3,2,1,0:T(8,128)(2,1)S(1)} %shard_map.158.mine_ref, bf16[3,4,64,256]{3,2,1,0:T(8,128)(2,1)S(1)} %collective-permute-done.3.other_ref, bf16[3,4,64,256]{3,2,1,0:T(8,128)(2,1)S(1)} %fusion.res_ref, f32[128,1]{1,0:T(8,128)S(1)} %copy.47.gain_ref, ...), custom_call_target="tpu_custom_call" | custom-call | flops 600000000 | bytes 2000000 | tf_op jit(solution)/shard_map/pallas_call | solution.py:181
  73.0 1.1 %copy.57 = bf16[3,64,4,256]{3,2,1,0:T(4,128)(2,1)} copy(bf16[3,64,4,256]{3,1,2,0:T(8,128)(2,1)S(1)} %bitcast.64) | data formatting | bytes 786432
  (69 shorter events, 1.5 us)
Async XLA Ops:
  1.3 15.0 %collective-permute-start.4 = (f32[4,256]{1,0:T(4,128)S(1)}, f32[4,256]{1,0:T(4,128)S(1)}, u32[]{:S(2)}, u32[]{:S(2)}) collective-permute-start(f32[4,256]{1,0:T(4,128)S(1)} %convert_multiply_fusion), channel_id=1, source_target_pairs={{0,16},{16,0},{1,17},{17,1},{2,18},{18,2},{3,19},{19,3},{4,20},{20... | collective-permute-start | bytes 12296 | tf_op jit(solution)/shard_map/ppermute | solution.py:234
  4.3 2.4 %copy-start.10 = (f32[4,4,2,128]{3,2,1,0:T(2,128)S(1)}, f32[4,4,2,128]{3,2,1,0:T(2,128)}, u32[]{:S(2)}) copy-start(f32[4,4,2,128]{3,2,1,0:T(2,128)} %param.19) | copy-start | bytes 49156
  6.1 2.7 %copy-start.1 = (bf16[2,96,4,2,128]{4,3,2,1,0:T(2,128)(2,1)S(1)}, bf16[2,96,4,2,128]{4,3,2,1,0:T(2,128)(2,1)}, u32[]{:S(2)}) copy-start(bf16[2,96,4,2,128]{4,3,2,1,0:T(2,128)(2,1)} %param.17) | copy-start | bytes 1179652
  6.6 13.4 %collective-permute-start.7 = (bf16[2,96,24]{1,0,2:T(2,128)(2,1)S(1)}, bf16[2,96,24]{1,0,2:T(2,128)(2,1)S(1)}, u32[]{:S(2)}, u32[]{:S(2)}) collective-permute-start(bf16[2,96,24]{1,0,2:T(2,128)(2,1)S(1)} %bitcast.76), channel_id=1, source_target_pairs={{0,16},{16,0},{1,17},{17,1},{2,18},{18,2},{3,19},{19,3},{4,20},{20... | collective-permute-start | bytes 27656 | tf_op jit(solution)/shard_map/ppermute | solution.py:236
  6.7 2.2 %copy-start.6 = (bf16[192,768]{1,0:T(8,128)(2,1)S(1)}, bf16[192,768]{1,0:T(8,128)(2,1)}, u32[]{:S(2)}) copy-start(bf16[192,768]{1,0:T(8,128)(2,1)} %param.26) | copy-start | bytes 884740
  6.7 12.9 %collective-permute-start = (f32[4,4,128]{2,1,0:T(4,128)S(1)}, f32[4,4,128]{2,1,0:T(4,128)S(1)}, u32[]{:S(2)}, u32[]{:S(2)}) collective-permute-start(f32[4,4,128]{2,1,0:T(4,128)S(1)} %bitcast.78), channel_id=1, source_target_pairs={{0,16},{16,0},{1,17},{17,1},{2,18},{18,2},{3,19},{19,3},{4,20},{20... | collective-permute-start | bytes 24584 | tf_op jit(solution)/shard_map/ppermute | solution.py:235
  9.1 0.8 %copy-start.12 = (f32[192]{0:T(256)S(1)}, f32[192]{0:T(256)}, u32[]{:S(2)}) copy-start(f32[192]{0:T(256)} %param.25) | copy-start | bytes 2308
  9.1 2.0 %copy-start.4 = (bf16[3,64,4,256]{3,2,1,0:T(4,128)(2,1)S(1)}, bf16[3,64,4,256]{3,2,1,0:T(4,128)(2,1)}, u32[]{:S(2)}) copy-start(bf16[3,64,4,256]{3,2,1,0:T(4,128)(2,1)} %param.15) | copy-start | bytes 1179652
  9.9 0.7 copy-start.14
  11.1 0.9 %copy-start.7 = (bf16[128,512]{1,0:T(8,128)(2,1)S(1)}, bf16[128,512]{1,0:T(8,128)(2,1)}, u32[]{:S(2)}) copy-start(bf16[128,512]{1,0:T(8,128)(2,1)} %param.22) | copy-start | bytes 393220
  12.1 0.9 %copy-start.3 = (bf16[512,128]{1,0:T(8,128)(2,1)S(1)}, bf16[512,128]{1,0:T(8,128)(2,1)}, u32[]{:S(2)}) copy-start(bf16[512,128]{1,0:T(8,128)(2,1)} %param.23) | copy-start | bytes 393220
  13.1 1.0 %copy-start.5 = (bf16[768,192]{0,1:T(8,128)(2,1)S(1)}, bf16[768,192]{0,1:T(8,128)(2,1)}, u32[]{:S(2)}) copy-start(bf16[768,192]{0,1:T(8,128)(2,1)} %param.27) | copy-start | bytes 884740
  14.3 0.7 copy-start.11
  14.3 0.7 copy-start
  14.3 0.9 %copy-start.8 = (f32[96,3,7,7]{0,3,2,1:T(8,128)S(1)}, f32[96,3,7,7]{0,3,2,1:T(8,128)}, u32[]{:S(2)}) copy-start(f32[96,3,7,7]{0,3,2,1:T(8,128)} %param.24) | copy-start | bytes 169348
  15.3 0.9 %copy-start.9 = (f32[64,3,7,7]{0,3,2,1:T(8,128)S(1)}, f32[64,3,7,7]{0,3,2,1:T(8,128)}, u32[]{:S(2)}) copy-start(f32[64,3,7,7]{0,3,2,1:T(8,128)} %param.20) | copy-start | bytes 112900
  16.3 0.7 copy-start.13
  17.2 2.5 %copy-start.15 = (f32[64]{0:T(128)S(1)}, f32[64]{0:T(128)}, u32[]{:S(2)}) copy-start(f32[64]{0:T(128)} %get-tuple-element.32) | copy-start | bytes 772
  17.3 2.6 %copy-start.2 = (f32[2,4,64,256]{3,2,1,0:T(8,128)S(1)}, f32[2,4,64,256]{3,2,1,0:T(8,128)}, u32[]{:S(2)}) copy-start(f32[2,4,64,256]{3,2,1,0:T(8,128)} %slice.120) | copy-start | bytes 1572868
  17.3 18.5 %collective-permute-start.6 = (bf16[2,2,3,96,128]{4,3,2,1,0:T(8,128)(2,1)S(1)}, bf16[2,2,3,96,128]{4,3,2,1,0:T(8,128)(2,1)S(1)}, u32[]{:S(2)}, u32[]{:S(2)}) collective-permute-start(bf16[2,2,3,96,128]{4,3,2,1,0:T(8,128)(2,1)S(1)} %get-tuple-element.11), channel_id=1, source_target_pairs={{2,0},{4,2},{6,4},{8,6},{10,8},{12,10},{14,12},{0,14},{3,1},{5,3},... | collective-permute-start | bytes 884744 | tf_op jit(solution)/shard_map/ppermute | solution.py:271
  19.5 16.3 %collective-permute-start.5 = (bf16[2,2,3,96,128]{4,3,2,1,0:T(8,128)(2,1)S(1)}, bf16[2,2,3,96,128]{4,3,2,1,0:T(8,128)(2,1)S(1)}, u32[]{:S(2)}, u32[]{:S(2)}) collective-permute-start(bf16[2,2,3,96,128]{4,3,2,1,0:T(8,128)(2,1)S(1)} %get-tuple-element.10), channel_id=1, source_target_pairs={{0,2},{2,4},{4,6},{6,8},{8,10},{10,12},{12,14},{14,0},{1,3},{3,5},... | collective-permute-start | bytes 884744 | tf_op jit(solution)/shard_map/ppermute | solution.py:270
  20.3 8.9 %collective-permute-start.9 = (bf16[2,96,36]{1,0,2:T(2,128)(2,1)S(1)}, bf16[2,96,36]{1,0,2:T(2,128)(2,1)S(1)}, u32[]{:S(2)}, u32[]{:S(2)}) collective-permute-start(bf16[2,96,36]{1,0,2:T(2,128)(2,1)S(1)} %bitcast.74), channel_id=1, source_target_pairs={{2,0},{4,2},{6,4},{8,6},{10,8},{12,10},{14,12},{0,14},{3,1},{5,3},... | collective-permute-start | bytes 41480 | tf_op jit(solution)/shard_map/ppermute | solution.py:274
  24.8 25.1 %collective-permute-start.1 = (bf16[3,3,64,256]{3,2,1,0:T(8,128)(2,1)}, bf16[3,3,64,256]{3,2,1,0:T(8,128)(2,1)}, u32[]{:S(2)}, u32[]{:S(2)}) collective-permute-start(bf16[3,3,64,256]{3,2,1,0:T(8,128)(2,1)} %get-tuple-element.12), channel_id=1, source_target_pairs={{0,2},{2,4},{4,6},{6,8},{8,10},{10,12},{12,14},{14,16},{16,18},{18... | collective-permute-start | bytes 884744 | tf_op jit(solution)/shard_map/ppermute | solution.py:250
  24.8 25.1 %collective-permute-start.2 = (bf16[3,3,64,256]{3,2,1,0:T(8,128)(2,1)}, bf16[3,3,64,256]{3,2,1,0:T(8,128)(2,1)}, u32[]{:S(2)}, u32[]{:S(2)}) collective-permute-start(bf16[3,3,64,256]{3,2,1,0:T(8,128)(2,1)} %get-tuple-element.13), channel_id=1, source_target_pairs={{2,0},{4,2},{6,4},{8,6},{10,8},{12,10},{14,12},{16,14},{18,16},{20... | collective-permute-start | bytes 884744 | tf_op jit(solution)/shard_map/ppermute | solution.py:251
  29.2 6.3 %collective-permute-start.8 = (bf16[2,96,36]{1,0,2:T(2,128)(2,1)S(1)}, bf16[2,96,36]{1,0,2:T(2,128)(2,1)S(1)}, u32[]{:S(2)}, u32[]{:S(2)}) collective-permute-start(bf16[2,96,36]{1,0,2:T(2,128)(2,1)S(1)} %bitcast.73), channel_id=1, source_target_pairs={{0,2},{2,4},{4,6},{6,8},{8,10},{10,12},{12,14},{14,0},{1,3},{3,5},... | collective-permute-start | bytes 41480 | tf_op jit(solution)/shard_map/ppermute | solution.py:273
  48.3 15.7 %collective-permute-start.10 = (bf16[2,2,4,96,128]{4,3,2,1,0:T(8,128)(2,1)S(1)}, bf16[2,2,4,96,128]{4,3,2,1,0:T(8,128)(2,1)S(1)}, u32[]{:S(2)}, u32[]{:S(2)}) collective-permute-start(bf16[2,2,4,96,128]{4,3,2,1,0:T(8,128)(2,1)S(1)} %shard_map.160), channel_id=1, source_target_pairs={{0,1},{1,0},{2,3},{3,2},{4,5},{5,4},{6,7},{7,6},{8,9},{9,8},{10,11... | collective-permute-start | bytes 1179656 | tf_op jit(solution)/shard_map/ppermute | solution.py:291
  61.9 7.8 %collective-permute-start.3 = (bf16[3,4,64,256]{3,2,1,0:T(8,128)(2,1)S(1)}, bf16[3,4,64,256]{3,2,1,0:T(8,128)(2,1)S(1)}, u32[]{:S(2)}, u32[]{:S(2)}) collective-permute-start(bf16[3,4,64,256]{3,2,1,0:T(8,128)(2,1)S(1)} %shard_map.158.mine_ref), channel_id=1, source_target_pairs={{0,1},{1,0},{2,3},{3,2},{4,5},{5,4},{6,7},{7,6},{8,9},{9,8},{10,11... | collective-permute-start | bytes 1179656 | tf_op jit(solution)/shard_map/ppermute | solution.py:286
